TPU v7x, 128 devices: a whole 4x4x4 slice. The times are simulated.
128 devices in a mesh: kv: 16 (over y, x), head: 8 (over z, core).
Axes of the slice: x: 4, y: 4, z: 4, core: 2. Of those that a mesh axis runs over, the one named last changes fastest.
Arguments:
- tokens: bfloat16 [128, 5120], P(None, 'kv'), may hold values from -6 to 6
- q_weight: bfloat16 [5120, 8192], P('kv', 'head'), may hold values from -0.078125 to 0.078125
- key_matrix: bfloat16 [5120, 1024], P('kv', 'head'), may hold values from -0.078125 to 0.078125
- value_matrix: bfloat16 [5120, 1024], P('kv', 'head'), may hold values from -0.078125 to 0.078125
- q_gain: float32 [64, 128], P('head'), may hold values from 0.4 to 45, as said below
- key_norm_scale: float32 [8, 128], P('head'), may hold values from 0.4 to 1.8
- stored_cache_keys: bfloat16 [32, 16384, 8, 128], P(None, 'kv', 'head'), may hold values from -6 to 6
- stored_cache_values: bfloat16 [32, 16384, 8, 128], P(None, 'kv', 'head'), may hold values from -6 to 6
- lengths: int32 [32], replicated, may hold values from 8 to 16384, as said below
- positions: int32 [32, 4], replicated, may hold values from 8 to 16387, as said below
- o_weight: bfloat16 [8192, 5120], P('head', 'kv'), may hold values from -0.0625 to 0.0625
Outputs:
- layer_out: bfloat16 [128, 5120], P('head', 'kv')
Inputs may be any that keep to these rules, and one draw needn't show every extreme that they name: `lengths`: every length is 8 or more; one request in each draw has exactly 16384 live positions. positions[r, 0] = lengths[r], and each later draft's position equals the previous one's or exceeds it by one; the request with 16384 live positions has its drafts at consecutive positions. `q_gain`: positive scales.
All inputs are finite; a program needn't handle non-finite values.
Results may differ from a plain program's by a relative error of at most 0.015.
Values may be sent and summed in bfloat16 or wider, within the bound.
A program may use at most 128 MiB of HBM per device.

v0:
```python
import math

import jax
import jax.numpy as jnp
from jax import lax
from jax.sharding import PartitionSpec as P

EPSILON = 1e-06
ROPE_BASE = 1000000.0
NEG = -1e30


def merged(part, axis, combine):
    gathered = jax.tree.map(lambda a: lax.all_gather(a, axis), part)

    def take(source):
        return jax.tree.map(lambda a: lax.dynamic_index_in_dim(a, source, 0, False), gathered)

    return lax.fori_loop(
        1, lax.axis_size(axis), lambda source, state: combine(state, take(source)), take(0)
    )


def norm_rotate(proj, gain, pos_rows):
    heads, head_dim = gain.shape
    count = proj.shape[0]
    vec = proj.reshape(count, heads, head_dim)
    vec = vec * lax.rsqrt(jnp.mean(vec * vec, axis=-1, keepdims=True) + EPSILON) * gain
    half = head_dim // 2
    freq = ROPE_BASE ** (-(jnp.arange(half, dtype=jnp.float32) * 2.0 / head_dim))
    angle = pos_rows.astype(jnp.float32)[:, None, None] * freq
    cosine = jnp.cos(angle)
    sine = jnp.sin(angle)
    first = vec[..., :half]
    second = vec[..., half:]
    out = jnp.concatenate([first * cosine - second * sine, second * cosine + first * sine], axis=-1)
    return out.reshape(count, heads * head_dim).astype(jnp.bfloat16)


def combine(left, right):
    peak = jnp.maximum(left[0], right[0])
    left_ratio = jnp.exp(left[0] - peak)
    right_ratio = jnp.exp(right[0] - peak)
    return (
        peak,
        left[1] * left_ratio + right[1] * right_ratio,
        left[2] * left_ratio[..., None] + right[2] * right_ratio[..., None],
    )


def on_device(
    tokens,
    q_weight,
    key_matrix,
    value_matrix,
    q_gain,
    key_norm_scale,
    stored_cache_keys,
    stored_cache_values,
    lengths,
    positions,
    o_weight,
):
    rows = tokens.shape[0]
    reqs, drafts = positions.shape
    pos_rows = positions.reshape(rows)
    q_part = jnp.dot(tokens, q_weight, preferred_element_type=jnp.float32)
    k_part = jnp.dot(tokens, key_matrix, preferred_element_type=jnp.float32)
    v_part = jnp.dot(tokens, value_matrix, preferred_element_type=jnp.float32)
    q_sum, k_sum, v_sum = lax.psum((q_part, k_part, v_part), "kv")
    query_rows = norm_rotate(q_sum, q_gain, pos_rows)
    incoming_keys = norm_rotate(k_sum, key_norm_scale, pos_rows)
    incoming_values = v_sum.astype(jnp.bfloat16)
    kv_local, head_dim = key_norm_scale.shape
    group_size = q_gain.shape[0] // kv_local
    query_blocks = query_rows.reshape(reqs, drafts, kv_local, group_size, head_dim)
    scale = 1.0 / math.sqrt(head_dim)
    local_len = stored_cache_keys.shape[1]
    width = min(512, local_len)
    count = local_len // width
    offset = lax.axis_index("kv") * local_len

    def absorb(carry, keys, values, live):
        top, total, acc = carry
        scores = (
            jnp.einsum("rjkgd,rtkd->rjkgt", query_blocks, keys, preferred_element_type=jnp.float32)
            * scale
        )
        mask = live[:, :, None, None, :]
        top_new = jnp.maximum(top, jnp.max(jnp.where(mask, scores, NEG), axis=-1))
        ratio = jnp.exp(top - top_new)
        weights = jnp.where(mask, jnp.exp(scores - top_new[..., None]), 0.0)
        total = total * ratio + jnp.sum(weights, axis=-1)
        acc = acc * ratio[..., None] + jnp.einsum(
            "rjkgt,rtkd->rjkgd",
            weights.astype(jnp.bfloat16),
            values,
            preferred_element_type=jnp.float32,
        )
        return (top_new, total, acc)

    def block_step(index, carry):
        start = index * width
        keys = lax.dynamic_slice_in_dim(stored_cache_keys, start, width, 1)
        values = lax.dynamic_slice_in_dim(stored_cache_values, start, width, 1)
        where_pos = offset + start + jnp.arange(width, dtype=jnp.int32)
        live = jnp.broadcast_to(
            (where_pos[None, :] < lengths[:, None])[:, None, :], (reqs, drafts, width)
        )
        return absorb(carry, keys, values, live)

    stat_shape = (reqs, drafts, kv_local, group_size)
    carry = (
        jnp.full(stat_shape, NEG, jnp.float32),
        jnp.zeros(stat_shape, jnp.float32),
        jnp.zeros(stat_shape + (head_dim,), jnp.float32),
    )
    carry = lax.fori_loop(0, count, block_step, carry)
    order = jnp.arange(drafts, dtype=jnp.int32)
    seen = (order[None, :] == order[:, None])[None] | (order[None, :] < order[:, None])[None] & (
        positions[:, None, :] < positions[:, :, None]
    )
    draft_live = seen & (lax.axis_index("kv") == 0)
    carry = absorb(
        carry,
        incoming_keys.reshape(reqs, drafts, kv_local, head_dim),
        incoming_values.reshape(reqs, drafts, kv_local, head_dim),
        draft_live,
    )
    heads_local = kv_local * group_size
    top, total, acc = merged(carry, "kv", combine)
    attended = (acc / total[..., None]).astype(jnp.bfloat16).reshape(rows, heads_local * head_dim)
    return lax.psum_scatter(
        jnp.dot(attended, o_weight, preferred_element_type=jnp.float32).astype(jnp.bfloat16),
        "head",
        scatter_dimension=0,
        tiled=True,
    )


def solution(mesh):
    placed = (
        P(None, "kv"),
        P("kv", "head"),
        P("kv", "head"),
        P("kv", "head"),
        P("head", None),
        P("head", None),
        P(None, "kv", "head", None),
        P(None, "kv", "head", None),
        P(),
        P(),
        P("head", "kv"),
    )
    return jax.shard_map(
        on_device, mesh=mesh, in_specs=placed, out_specs=P("head", "kv"), check_vma=False
    )
```

profile of v0, /device:TPU:1, one launch (start us, length us, event | category | flops | bytes accessed | tf_op | source)
XLA Modules:
  0.0 255.8 jit_solution(5746890083174574235)
XLA Ops:
  6.6 1.8 fusion.55
  8.4 1.2 convolution_bitcast_fusion.1
  11.2 61.4 %psum.23 = bf16[128,128]{1,0:T(8,128)(2,1)S(1)} all-reduce(f32[128,128]{1,0:T(8,128)S(1)} %fusion.56), channel_id=1, replica_groups=mesh['kv'=16,'head'=8] {'kv'}, use_global_device_ids=true, to_apply=%region_10.11 | all-reduce | flops 16384 | bytes 98304 | tf_op jit(solution)/shard_map/psum | solution.py:70
  73.0 24.6 %all-reduce.3.cloned.1.call-done = (f32[128,128]{0,1:T(8,128)}, f32[128,8,128]{2,1,0:T(8,128)}) async-done(((f32[128,128]{0,1:T(8,128)}, f32[128,8,128]{2,1,0:T(8,128)}), (f32[128,128]{0,1:T(8,128)}, f32[128,8,128]{2,1,0:T(8,128)})) %all-reduce.3.cloned.1.call-update) | async-done | bytes 589840 | tf_op jit(solution)/shard_map/psum | solution.py:70
  99.7 1.3 multiply_reduce_fusion
  101.2 1.2 multiply_multiply_fusion
  102.9 12.1 %while.38 = (s32[]{:T(128)}, f32[32,4,1,8]{3,1,0,2:T(4,128)S(1)}, f32[32,4,1,8]{3,1,0,2:T(4,128)S(1)}, f32[32,4,1,8,128]{4,3,1,0,2:T(8,128)S(1)}, s32[]{:T(128)}...) while((s32[]{:T(128)}, f32[32,4,1,8]{3,1,0,2:T(4,128)S(1)}, ...), condition=%wide.region_5.6_spmd.clone, body=%wide.region_2.5_spmd.clone.sunk | while | flops 274618880 | bytes 49803632 | solution.py:118
  103.0 4.0 %fusion.80 = (f32[32,4,8]{2,1,0:T(4,128)S(1)}, f32[32,512,4,8]{1,3,2,0:T(8,128)S(1)}) fusion(pred[32,512]{1,0:T(8,128)(4,1)S(1)} %broadcast_compare_fusion.2, bf16[32,4,1,8,128]{4,3,1,0,2:T(8,128)(2,1)S(1)} %get-tuple-element.670, bf16[32,1024,1,128]{3,1,0,2:T(8,128)(2,1)} %get-tuple-element.669, s32[]{:T(128)S(6)} %select_n.86), kind=kOutput, calls=%fused_computation.20.clone.1 | convolution fusion | flops 135789568 | bytes 6574084 | tf_op jit(solution)/shard_map/while/body/eval_jaxpr/rjkgd,rtkd->rjkgt/dot_general | solution.py:86
  109.1 3.9 %fusion.80 = (f32[32,4,8]{2,1,0:T(4,128)S(1)}, f32[32,512,4,8]{1,3,2,0:T(8,128)S(1)}) fusion(pred[32,512]{1,0:T(8,128)(4,1)S(1)} %broadcast_compare_fusion.2, bf16[32,4,1,8,128]{4,3,1,0,2:T(8,128)(2,1)S(1)} %get-tuple-element.670, bf16[32,1024,1,128]{3,1,0,2:T(8,128)(2,1)} %get-tuple-element.669, s32[]{:T(128)S(6)} %select_n.86), kind=kOutput, calls=%fused_computation.20.clone.1 | convolution fusion | flops 135789568 | bytes 6574084 | tf_op jit(solution)/shard_map/while/body/eval_jaxpr/rjkgd,rtkd->rjkgt/dot_general | solution.py:86
  113.9 1.1 fusion.82
  115.1 1.3 select_reduce_fusion
  116.4 1.5 fusion.33
  118.0 20.4 %all-gather = f32[512,4,1,8]{3,1,2,0:T(4,128)S(1)} all-gather(f32[32,4,1,8]{3,1,2,0:T(4,128)S(1)} %get-tuple-element.508), channel_id=2, replica_groups=mesh['kv'=16,'head'=8] {'kv'}, dimensions={0}, use_global_device_ids=true | all-gather | bytes 69632 | tf_op jit(solution)/shard_map/all_gather | solution.py:14
  139.2 17.8 %all-gather.1 = f32[512,4,1,8]{3,1,2,0:T(4,128)S(1)} all-gather(f32[32,4,1,8]{3,1,2,0:T(4,128)S(1)} %bitcast_add_fusion.1), channel_id=3, replica_groups=mesh['kv'=16,'head'=8] {'kv'}, dimensions={0}, use_global_device_ids=true | all-gather | bytes 69632 | tf_op jit(solution)/shard_map/all_gather | solution.py:14
  157.4 36.1 %all-gather.5.cloned.1.call-done = f32[512,4,1,8,128]{4,3,2,1,0:T(8,128)} async-done(((f32[32,4,1,8,128]{4,3,2,1,0:T(8,128)}), f32[512,4,1,8,128]{4,3,2,1,0:T(8,128)}) %all-gather.5.cloned.1.call-update) | async-done | bytes 8388624 | tf_op jit(solution)/shard_map/all_gather | solution.py:14
  194.7 25.7 %while.37 = (s32[]{:T(128)}, f32[32,4,1,8]{0,3,2,1:T(8,128)S(1)}, f32[32,4,1,8]{0,3,2,1:T(8,128)S(1)}, f32[32,4,1,8,128]{4,3,2,1,0:T(8,128)S(1)}, f32[16,32,4,1,...) while((s32[]{:T(128)}, f32[32,4,1,8]{0,3,2,1:T(8,128)S(1)}, ...), condition=%wide.region_12.13_spmd, body=%wide.region_11.12_spmd.sunk | while | flops 400389 | bytes 1650835 | solution.py:19
  194.9 1.4 fusion.77
  196.6 1.4 fusion.77
  198.3 1.4 fusion.77
  200.1 1.4 fusion.77
  201.8 1.4 fusion.77
  203.5 1.4 fusion.77
  205.2 1.4 fusion.77
  206.9 1.4 fusion.77
  208.6 1.4 fusion.77
  210.3 1.4 fusion.77
  212.0 1.4 fusion.77
  213.7 1.4 fusion.77
  215.5 1.4 fusion.77
  217.2 1.4 fusion.77
  218.9 1.4 fusion.77
  221.7 27.6 %reduce-scatter.2.cloned.1.call-done = bf16[16,320]{1,0:T(8,128)(2,1)} async-done(((bf16[128,320]{1,0:T(8,128)(2,1)}), bf16[16,320]{1,0:T(8,128)(2,1)}) %reduce-scatter.2.cloned.1.call-update) | async-done | bytes 10256 | tf_op jit(solution)/shard_map/reduce_scatter | solution.py:133
  (151 shorter events, 14.6 us)
Async XLA Ops:
  6.5 1.9 copy-start
  6.5 4.4 %copy-start.1 = (bf16[128,320]{0,1:T(8,128)(2,1)S(1)}, bf16[128,320]{0,1:T(8,128)(2,1)}, u32[]{:S(2)}) copy-start(bf16[128,320]{0,1:T(8,128)(2,1)} %param.15) | copy-start | bytes 245764
  6.5 4.1 %copy-start.5 = (s32[32,4]{0,1:T(4,128)S(1)}, s32[32,4]{0,1:T(4,128)}, u32[]{:S(2)}) copy-start(s32[32,4]{0,1:T(4,128)} %param.24) | copy-start | bytes 1540
  6.5 4.4 %copy-start.3 = (bf16[320,128]{1,0:T(8,128)(2,1)S(1)}, bf16[320,128]{1,0:T(8,128)(2,1)}, u32[]{:S(2)}) copy-start(bf16[320,128]{1,0:T(8,128)(2,1)} %param.18) | copy-start | bytes 245764
  6.5 91.9 %copy-start.7 = (f32[1,128]{1,0:T(1,128)S(1)}, f32[1,128]{1,0:T(1,128)}, u32[]{:S(2)}) copy-start(f32[1,128]{1,0:T(1,128)} %param.20) | copy-start | bytes 1540
  6.5 91.0 %all-reduce.3.cloned.1.call-start = ((), (), s32[]{:S(2)}) async-start(), calls=%async_computation.3 | async-start | bytes 1179648 | tf_op jit(solution)/shard_map/psum | solution.py:70
  8.4 92.7 %copy-start.6 = (f32[8,128]{1,0:T(8,128)S(1)}, f32[8,128]{1,0:T(8,128)}, u32[]{:S(2)}) copy-start(f32[8,128]{1,0:T(8,128)} %param.19) | copy-start | bytes 12292
  10.6 183.0 %all-gather.5.cloned.1.call-start = ((), (), s32[]{:S(2)}) async-start(), calls=%async_computation.2 | async-start | bytes 8912896 | tf_op jit(solution)/shard_map/all_gather | solution.py:14
  99.7 3.2 %copy-start.4 = (s32[32]{0:T(128)S(1)}, s32[32]{0:T(128)}, u32[]{:S(2)}) copy-start(s32[32]{0:T(128)} %param.23) | copy-start | bytes 388
  103.0 4.8 %copy-start.8 = (bf16[32,1024,1,128]{3,1,0,2:T(8,128)(2,1)S(1)}, bf16[32,1024,1,128]{3,1,0,2:T(8,128)(2,1)}, u32[]{:S(2)}) copy-start(bf16[32,1024,1,128]{3,1,0,2:T(8,128)(2,1)} %get-tuple-element.671) | copy-start | bytes 25165828 | tf_op jit(solution)/shard_map/while
  109.1 4.8 %copy-start.8 = (bf16[32,1024,1,128]{3,1,0,2:T(8,128)(2,1)S(1)}, bf16[32,1024,1,128]{3,1,0,2:T(8,128)(2,1)}, u32[]{:S(2)}) copy-start(bf16[32,1024,1,128]{3,1,0,2:T(8,128)(2,1)} %get-tuple-element.671) | copy-start | bytes 25165828 | tf_op jit(solution)/shard_map/while
  117.9 131.3 %reduce-scatter.2.cloned.1.call-start = ((), (), s32[]{:S(2)}) async-start(), calls=%async_computation.1 | async-start | bytes 110592 | tf_op jit(solution)/shard_map/reduce_scatter | solution.py:133
  194.6 26.0 %copy-start.2 = (bf16[1024,320]{0,1:T(8,128)(2,1)S(1)}, bf16[1024,320]{0,1:T(8,128)(2,1)}, u32[]{:S(2)}) copy-start(bf16[1024,320]{0,1:T(8,128)(2,1)} %param.25) | copy-start | bytes 1966084
Sparse Core Ops, SparseCore 0:
  10.7 86.8 all-reduce.2
  118.1 75.4 all-gather.4
  221.8 27.4 reduce-scatter.1
where the time goes:
time: 259 us; the launch traced here: 256 us
  blocking collectives  99.6 us (38%)
  waiting for transfers between devices  88.3 us (34%)
  other arithmetic  30.1 us (12%)
  matrix products  17.1 us (7%)
  between operations  13.4 us (5%)
  local copies, waits for them, and re-layouts  6.09 us (2%)
    psum x1, blocking collectives, on_device(): q_sum, k_sum, v_sum = lax.psum((q_part, k_part, v_part), 'kv')  61.4 us
    all_gather x2, blocking collectives, merged(): gathered = jax.tree.map(lambda a: lax.all_gather(a, axis), part)  38.2 us
    all_gather x1, waiting for transfers between devices, merged(): gathered = jax.tree.map(lambda a: lax.all_gather(a, axis), part)  36.1 us
    reduce_scatter x1, waiting for transfers between devices, on_device(): lax.psum_scatter(jnp.dot(attended, o_weight, preferred_element_type=jnp.f...  27.6 us
    psum x1, waiting for transfers between devices, on_device(): q_sum, k_sum, v_sum = lax.psum((q_part, k_part, v_part), 'kv')  24.6 us
    add x15, other arithmetic, combine(): left[2] * left_ratio[..., None] + right[2] * right_ratio[..., None]  21.6 us
    dot_general x3, matrix products, absorb(): jnp.einsum('rjkgd,rtkd->rjkgt', query_blocks, keys, preferred_element_typ...  9.19 us
  transfers between devices with their start and end apart: 3, of which 3 were waited for; matrix products, arithmetic and copies ran while one was open for 1% of the time, Pallas kernels for 0%

commit v1 on v0

v1 whole, which is shorter than its diff:
```python
import functools
import math

import jax
import jax.numpy as jnp
import numpy as np
from jax import lax
from jax.experimental import pallas as pl
from jax.experimental.pallas import tpu as pltpu
from jax.sharding import PartitionSpec as P

EPSILON = 1e-06
ROPE_BASE = 1000000.0
NEG = -1e30
MESH = pl.DeviceIdType.MESH


def column_to_row(col):
    rows = col.shape[0]
    wide = jnp.broadcast_to(col, (rows, 128))
    row_id = lax.broadcasted_iota(jnp.int32, (rows, 128), 0)
    lane_id = lax.broadcasted_iota(jnp.int32, (rows, 128), 1)
    return jnp.sum(jnp.where(row_id == lane_id, wide, 0.0), axis=0, keepdims=True)


def kernel(
    nk, side, nh, drafts,
    tokens, q_weight, key_matrix, value_matrix, q_gain, k_gain, keys, values, o_weight, freq,
    lengths, positions,
    out,
    tok_v, wq_v, wk_v, wv_v, qg_v, kg_v, wo_v, freq_v, keys_v, values_v,
    part, part_in, query, attn, attn_in, lse, lse_in, attended, proj, proj_in,
    load_sem, key_sem, value_sem, part_ss, part_rs, query_ss, query_rs,
    attn_ss, attn_rs, lse_ss, lse_rs, att_ss, att_rs, proj_ss, proj_rs,
):
    me = lax.axis_index("kv")
    my_head = lax.axis_index("head")
    my_y, my_x = me // side, me % side
    reqs, local_len, head_dim = keys.shape
    rows = tokens.shape[1]
    heads = q_gain.shape[0]
    per = reqs // nk
    own = per * drafts
    group = heads * drafts
    scale = 1.0 / math.sqrt(head_dim)
    to_log2 = scale * math.log2(math.e)

    def ahead(s):
        return lax.rem(my_y + s // side, side) * side + lax.rem(my_x + s % side, side)

    def behind(s):
        return (
            lax.rem(my_y + side - s // side, side) * side + lax.rem(my_x + side - s % side, side)
        )

    barrier = pltpu.get_barrier_semaphore()
    for s in range(1, nk):
        pl.semaphore_signal(barrier, inc=1, device_id={"kv": ahead(s)}, device_id_type=MESH)
    for s in range(1, nh):
        pl.semaphore_signal(
            barrier, inc=1, device_id={"head": lax.rem(my_head + s, nh)}, device_id_type=MESH
        )

    loads = [
        pltpu.make_async_copy(src, dst, load_sem.at[n])
        for n, (src, dst) in enumerate(
            [
                (tokens, tok_v), (q_weight, wq_v), (key_matrix, wk_v), (value_matrix, wv_v),
                (q_gain, qg_v), (k_gain, kg_v), (freq, freq_v), (o_weight, wo_v),
            ]
        )
    ]
    for copy in loads:
        copy.start()

    def cache_copies(s):
        at = pl.ds(per * behind(s), per)
        slot = pl.ds(per * s, per)
        return (
            pltpu.make_async_copy(keys.at[at], keys_v.at[slot], key_sem.at[s]),
            pltpu.make_async_copy(values.at[at], values_v.at[slot], value_sem.at[s]),
        )

    @pl.loop(0, nk)
    def _(s):
        for copy in cache_copies(s):
            copy.start()

    for copy in loads[:4]:
        copy.wait()
    toks = tok_v[...]
    for h in range(heads + 2):
        if h < heads:
            weight = wq_v[:, h * head_dim : (h + 1) * head_dim]
        else:
            weight = (wk_v if h == heads else wv_v)[...]
        part[:, h * own : (h + 1) * own, :] = lax.dot_general(
            toks, weight, (((0,), (0,)), ((), ())), preferred_element_type=jnp.float32
        ).reshape(nk, own, head_dim)

    pl.semaphore_wait(barrier, nk + nh - 2)

    def part_copy(s):
        return pltpu.make_async_remote_copy(
            src_ref=part.at[ahead(s)], dst_ref=part_in.at[s],
            send_sem=part_ss.at[s], recv_sem=part_rs.at[s],
            device_id={"kv": ahead(s)}, device_id_type=MESH,
        )

    @pl.loop(1, nk)
    def _(s):
        part_copy(s).start()

    for copy in loads[4:]:
        copy.wait()
    row_id = lax.broadcasted_iota(jnp.int32, (own, head_dim), 0)
    lane_id = lax.broadcasted_iota(jnp.int32, (own, head_dim), 1)
    place = [[positions[j, per * me + r] for j in range(drafts)] for r in range(per)]
    place_rows = jnp.zeros((own, head_dim), jnp.int32)
    for r in range(per):
        for j in range(drafts):
            place_rows = jnp.where(row_id == r * drafts + j, place[r][j], place_rows)
    angle = place_rows.astype(jnp.float32) * freq_v[...]
    cosine = jnp.cos(angle)
    sine = jnp.sin(angle)
    sine = jnp.where(lane_id < head_dim // 2, -sine, sine)
    fresh_row = lax.broadcasted_iota(jnp.int32, (per * group, 16), 0)
    fresh_col = lax.broadcasted_iota(jnp.int32, (per * group, 16), 1)
    seen = fresh_row < 0
    for r in range(per):
        for j in range(drafts):
            here = (fresh_row // group == r) & (fresh_row % drafts == j)
            for i in range(j + 1):
                hit = here & (fresh_col == r * drafts + i)
                if i < j:
                    hit = hit & (place[r][i] < place[r][j])
                seen = seen | hit

    @pl.loop(1, nk)
    def _(s):
        part_copy(s).wait_recv()

    raw = part[me]
    for s in range(1, nk):
        raw = raw + part_in[s]
    raw = raw.reshape(heads + 2, own, head_dim)

    def norm_rotate(vec, gain):
        vec = vec * lax.rsqrt(jnp.mean(vec * vec, axis=-1, keepdims=True) + EPSILON) * gain
        turned = pltpu.roll(vec.reshape(-1, head_dim), head_dim // 2, 1).reshape(vec.shape)
        return vec * cosine[None] + turned * sine[None]

    queries = norm_rotate(raw[:heads], qg_v[...][:, None, :])
    queries = jnp.swapaxes(queries.reshape(heads, per, drafts, head_dim), 0, 1)
    queries = queries.reshape(per * group, head_dim).astype(jnp.bfloat16)
    query[0] = queries

    def query_copy(s):
        return pltpu.make_async_remote_copy(
            src_ref=query.at[0], dst_ref=query.at[s],
            send_sem=query_ss.at[s], recv_sem=query_rs.at[s],
            device_id={"kv": ahead(s)}, device_id_type=MESH,
        )

    @pl.loop(1, nk)
    def _(s):
        query_copy(s).start()

    fresh_k = norm_rotate(raw[heads : heads + 1], kg_v[...][:, None, :]).reshape(own, head_dim)
    pad = jnp.zeros((16 - own, head_dim), jnp.float32)
    fresh_k = jnp.concatenate([fresh_k, pad], axis=0).astype(jnp.bfloat16)
    fresh_v = jnp.concatenate([raw[heads + 1], pad], axis=0).astype(jnp.bfloat16)

    def softmax_part(scores, vals):
        top = jnp.max(scores, axis=-1, keepdims=True)
        weights = jnp.exp2((scores - top) * to_log2)
        total = jnp.sum(weights, axis=-1, keepdims=True)
        mixed = jnp.dot(weights.astype(jnp.bfloat16), vals, preferred_element_type=jnp.float32)
        return mixed / total, top * to_log2 + jnp.log2(total)

    def dot_t(left, right):
        return lax.dot_general(
            left, right, (((1,), (1,)), ((), ())), preferred_element_type=jnp.float32
        )

    fresh_out, fresh_lse = softmax_part(
        jnp.where(seen, dot_t(queries, fresh_k), NEG), fresh_v
    )
    fresh_lse = column_to_row(fresh_lse)

    def attn_copies(s):
        return (
            pltpu.make_async_remote_copy(
                src_ref=attn.at[s], dst_ref=attn_in.at[s],
                send_sem=attn_ss.at[s], recv_sem=attn_rs.at[s],
                device_id={"kv": behind(s)}, device_id_type=MESH,
            ),
            pltpu.make_async_remote_copy(
                src_ref=lse.at[s], dst_ref=lse_in.at[s],
                send_sem=lse_ss.at[s], recv_sem=lse_rs.at[s],
                device_id={"kv": behind(s)}, device_id_type=MESH,
            ),
        )

    spot = me * local_len + lax.broadcasted_iota(jnp.int32, (1, local_len), 1)

    @pl.loop(0, nk)
    def _(s):
        @pl.when(s > 0)
        def _():
            query_copy(s).wait_recv()

        for copy in cache_copies(s):
            copy.wait()
        block = query[s]
        outs, stats = [], []
        for r in range(per):
            live = spot < lengths[per * behind(s) + r]
            scores = dot_t(block[r * group : (r + 1) * group], keys_v[per * s + r])
            mixed, stat = softmax_part(jnp.where(live, scores, NEG), values_v[per * s + r])
            outs.append(mixed)
            stats.append(stat)
        attn[s] = jnp.concatenate(outs, axis=0).astype(jnp.bfloat16)
        lse[s] = column_to_row(jnp.concatenate(stats, axis=0))

        @pl.when(s > 0)
        def _():
            for copy in attn_copies(s):
                copy.start()

    @pl.loop(1, nk)
    def _(s):
        for copy in attn_copies(s):
            copy.wait_recv()

    stats = jnp.concatenate([lse[0], fresh_lse] + [lse_in[s] for s in range(1, nk)], axis=0)
    ratio = jnp.exp2(stats - jnp.max(stats, axis=0, keepdims=True))
    ratio = ratio / jnp.sum(ratio, axis=0, keepdims=True)
    ratio = jnp.concatenate([ratio, jnp.zeros((128 - nk - 1, 128), jnp.float32)], axis=0).T
    ratio = ratio[: per * group]
    merged = attn[0].astype(jnp.float32) * ratio[:, 0:1] + fresh_out * ratio[:, 1:2]
    for s in range(1, nk):
        merged = merged + attn_in[s].astype(jnp.float32) * ratio[:, s + 1 : s + 2]
    merged = jnp.swapaxes(merged.reshape(per, heads, drafts, head_dim), 0, 1)
    attended[me] = merged.reshape(heads * own, head_dim).astype(jnp.bfloat16)

    def att_copy(s):
        return pltpu.make_async_remote_copy(
            src_ref=attended.at[me], dst_ref=attended.at[me],
            send_sem=att_ss.at[s], recv_sem=att_rs.at[s],
            device_id={"kv": ahead(s)}, device_id_type=MESH,
        )

    def att_arrival(s):
        return pltpu.make_async_remote_copy(
            src_ref=attended.at[me], dst_ref=attended.at[behind(s)],
            send_sem=att_ss.at[s], recv_sem=att_rs.at[s],
            device_id={"kv": ahead(s)}, device_id_type=MESH,
        )

    @pl.loop(1, nk)
    def _(s):
        att_copy(s).start()

    @pl.loop(1, nk)
    def _(s):
        att_arrival(s).wait_recv()

    total = None
    for h in range(0, heads, 2):
        pair = attended[:, h * own : (h + 2) * own, :].astype(jnp.float32)
        pair = pair.reshape(nk, 2, own, head_dim)
        for k in range(2):
            side_in = pair[:, k].reshape(rows, head_dim).astype(jnp.bfloat16)
            term = dot_t(side_in, wo_v[:, (h + k) * head_dim : (h + k + 1) * head_dim])
            total = term if total is None else total + term
    proj[...] = total.astype(jnp.bfloat16).reshape(proj.shape)

    def proj_copy(s):
        target = lax.rem(my_head + s, nh)
        return pltpu.make_async_remote_copy(
            src_ref=proj.at[target], dst_ref=proj_in.at[s],
            send_sem=proj_ss.at[s], recv_sem=proj_rs.at[s],
            device_id={"head": target}, device_id_type=MESH,
        )

    for s in range(1, nh):
        proj_copy(s).start()
    for s in range(1, nh):
        proj_copy(s).wait_recv()
    result = proj[my_head].astype(jnp.float32)
    for s in range(1, nh):
        result = result + proj_in[s].astype(jnp.float32)
    out[...] = result.astype(jnp.bfloat16)

    @pl.loop(1, nk)
    def _(s):
        part_copy(s).wait_send()
        query_copy(s).wait_send()
        for copy in attn_copies(s):
            copy.wait_send()
        att_copy(s).wait_send()

    for s in range(1, nh):
        proj_copy(s).wait_send()


def on_device(
    nk, nh,
    tokens, q_weight, key_matrix, value_matrix, q_gain, k_gain, keys, values, lengths, positions,
    o_weight,
):
    rows = tokens.shape[0]
    reqs, drafts = positions.shape
    width = o_weight.shape[1]
    tokens, o_weight, positions = tokens.T, o_weight.T, positions.T
    _, local_len, _, head_dim = keys.shape
    keys = keys.reshape(reqs, local_len, head_dim)
    values = values.reshape(reqs, local_len, head_dim)
    heads = q_gain.shape[0]
    side = math.isqrt(nk)
    own = rows // nk
    block = rows // nh
    exponent = np.arange(head_dim // 2, dtype=np.float64) * 2.0 / head_dim
    freq = np.tile((ROPE_BASE ** -exponent).astype(np.float32), 2)[None]
    bf16, f32 = jnp.bfloat16, jnp.float32
    dma = pltpu.SemaphoreType.DMA
    hbm = pl.BlockSpec(memory_space=pltpu.HBM)
    smem = pl.BlockSpec(memory_space=pltpu.SMEM)
    return pl.pallas_call(
        functools.partial(kernel, nk, side, nh, drafts),
        out_shape=jax.ShapeDtypeStruct((block, width), bf16),
        in_specs=[hbm] * 10 + [smem] * 2,
        out_specs=pl.BlockSpec(memory_space=pltpu.VMEM),
        scratch_shapes=[
            pltpu.VMEM(tokens.shape, bf16),
            pltpu.VMEM(q_weight.shape, bf16),
            pltpu.VMEM(key_matrix.shape, bf16),
            pltpu.VMEM(value_matrix.shape, bf16),
            pltpu.VMEM(q_gain.shape, f32),
            pltpu.VMEM(k_gain.shape, f32),
            pltpu.VMEM(o_weight.shape, bf16),
            pltpu.VMEM(freq.shape, f32),
            pltpu.VMEM(keys.shape, bf16),
            pltpu.VMEM(values.shape, bf16),
            pltpu.VMEM((nk, (heads + 2) * own, head_dim), f32),
            pltpu.VMEM((nk, (heads + 2) * own, head_dim), f32),
            pltpu.VMEM((nk, heads * own, head_dim), bf16),
            pltpu.VMEM((nk, heads * own, head_dim), bf16),
            pltpu.VMEM((nk, heads * own, head_dim), bf16),
            pltpu.VMEM((nk, 1, 128), f32),
            pltpu.VMEM((nk, 1, 128), f32),
            pltpu.VMEM((nk, heads * own, head_dim), bf16),
            pltpu.VMEM((nh, block, width), bf16),
            pltpu.VMEM((nh, block, width), bf16),
            dma((8,)),
        ]
        + [dma((nk,))] * 12
        + [dma((nh,))] * 2,
        compiler_params=pltpu.CompilerParams(
            collective_id=0, has_side_effects=True, vmem_limit_bytes=60 * 1024 * 1024
        ),
    )(
        tokens, q_weight, key_matrix, value_matrix, q_gain, k_gain, keys, values, o_weight,
        jnp.asarray(freq), lengths, positions,
    )


def solution(mesh):
    placed = (
        P(None, "kv"),
        P("kv", "head"),
        P("kv", "head"),
        P("kv", "head"),
        P("head", None),
        P("head", None),
        P(None, "kv", "head", None),
        P(None, "kv", "head", None),
        P(),
        P(),
        P("head", "kv"),
    )
    return jax.shard_map(
        functools.partial(on_device, mesh.shape["kv"], mesh.shape["head"]),
        mesh=mesh,
        in_specs=placed,
        out_specs=P("head", "kv"),
        check_vma=False,
    )
```

time: 259 us -> 53.2 us (0.21); the launches traced: 256 us -> 53.1 us
  blocking collectives: 99.6 us -> 0 us
  waiting for transfers between devices: 88.3 us -> 0 us
  Pallas kernels: 0 us -> 51.7 us
  other arithmetic: 30.1 us -> 0 us
  matrix products: 17.1 us -> 0 us
  between operations: 13.4 us -> 0.01 us
  local copies, waits for them, and re-layouts: 6.09 us -> 1.31 us
    psum x1 -> x0, blocking collectives: 61.4 us -> none  [on_device(): q_sum, k_sum, v_sum = lax.psum((q_part, k_part, v_part), 'kv')]
    pallas_call x0 -> x1, Pallas kernels: none -> 51.7 us  [on_device(): pl.pallas_call(functools.partial(kernel, nk, side, nh, drafts), out_shape...]
    all_gather x2 -> x0, blocking collectives: 38.2 us -> none  [merged(): gathered = jax.tree.map(lambda a: lax.all_gather(a, axis), part)]
    all_gather x1 -> x0, waiting for transfers between devices: 36.1 us -> none  [merged(): gathered = jax.tree.map(lambda a: lax.all_gather(a, axis), part)]
    reduce_scatter x1 -> x0, waiting for transfers between devices: 27.6 us -> none  [on_device(): lax.psum_scatter(jnp.dot(attended, o_weight, preferred_element_type=jnp.f...]
    psum x1 -> x0, waiting for transfers between devices: 24.6 us -> none  [on_device(): q_sum, k_sum, v_sum = lax.psum((q_part, k_part, v_part), 'kv')]
    add x20 -> x0, other arithmetic: 21.8 us -> none  [the longest x15 21.6 us: combine(): left[2] * left_ratio[..., None] + right[2] * right_ratio[..., None]]
    dot_general x10 -> x0, matrix products: 17.1 us -> none  [the longest x3 9.19 us: absorb(): jnp.einsum('rjkgd,rtkd->rjkgt', query_blocks, keys, preferred_element_typ...]
  transfers between devices with their start and end apart: 3 -> 0, of which waited for: 3 -> 0; matrix products, arithmetic and copies ran while one was open for 1% -> 0% of each run, Pallas kernels for 0% -> 0%
where the time goes in v1:
time: 53.2 us; the launch traced here: 53.1 us
  Pallas kernels  51.7 us (97%)
  local copies, waits for them, and re-layouts  1.31 us (2%)
    pallas_call x1, Pallas kernels, on_device(): pl.pallas_call(functools.partial(kernel, nk, side, nh, drafts), out_shape...  51.7 us
    unnamed x1, local copies, waits for them, and re-layouts  1.31 us

profile of v1, /device:TPU:1, one launch (start us, length us, event | category | flops | bytes accessed | tf_op | source)
XLA Modules:
  0.0 53.1 jit_solution(11279126978392660676)
XLA Ops:
  0.0 51.7 %shard_map.118 = bf16[16,320]{1,0:T(8,128)(2,1)} custom-call(bf16[320,128]{1,0:T(8,128)(2,1)} %bitcast.8, bf16[320,1024]{1,0:T(8,128)(2,1)} %q_weight.1, bf16[320,128]{1,0:T(8,128)(2,1)} %key_matrix.1, bf16[320,128]{1,0:T(8,128)(2,1)} %value_matrix.1, f32[8,128]{1,0:T(8,128)} %q_gain.1, f32[1,128]{1,0:T(1,128)} %k_gain.1, bf16[32,1024,128]{2,1,0:T(8,128)(2,1)} %bitcast.5, ...), custom_call_target="tpu_custom_call" | custom-call | tf_op jit(solution)/shard_map/pallas_call | solution.py:330
  51.8 1.3 %copy.14 = bf16[16,320]{1,0:T(8,128)(2,1)} copy(bf16[16,320]{1,0:T(8,128)(2,1)} %shard_map.118) | data formatting | bytes 20480

commit v2 on v1

v2 whole, which is shorter than its diff:
```python
import functools
import math

import jax
import jax.numpy as jnp
import numpy as np
from jax import lax
from jax.experimental import pallas as pl
from jax.experimental.pallas import tpu as pltpu
from jax.sharding import PartitionSpec as P

EPSILON = 1e-06
ROPE_BASE = 1000000.0
NEG = -1e30
MESH = pl.DeviceIdType.MESH


def column_to_row(col):
    rows = col.shape[0]
    wide = jnp.broadcast_to(col, (rows, 128))
    row_id = lax.broadcasted_iota(jnp.int32, (rows, 128), 0)
    lane_id = lax.broadcasted_iota(jnp.int32, (rows, 128), 1)
    return jnp.sum(jnp.where(row_id == lane_id, wide, 0.0), axis=0, keepdims=True)


def schedule(side):
    far = lambda at: sum(min(d, side - d) for d in at)
    spots = [(y, x) for y in range(side) for x in range(side)]
    ring = [[at for at in spots if far(at) == n] for n in range(side + 1)]
    batches = [
        ring[0] + ring[1][:-1],
        ring[2][:4],
        [at for n in range(side, 2, -1) for at in ring[n]],
        ring[2][4:] + ring[1][-1:],
    ]
    return [batch for batch in batches if batch]


def drain(ref, sem):
    pltpu.make_async_copy(ref, ref, sem).wait()


def kernel(
    nk, side, nh, drafts, batches,
    tokens, q_weight, key_matrix, value_matrix, q_gain, k_gain, keys, values, o_weight, freq,
    lengths_in, positions_in,
    out,
    tok_v, wq_v, wk_v, wv_v, qg_v, kg_v, wo_v, freq_v, keys_v, values_v, lengths, positions,
    part, part_in, query, attn, attn_in, lse, lse_in, attended, proj, proj_in,
    load_sem, key_sem, value_sem, query_rs, sems,
):
    (part_ss, part_rs, fresh_rs, query_ss, attn_ss, attn_rs, lse_ss, lse_rs, att_ss, att_rs,
     proj_ss, proj_rs) = [sems.at[n] for n in range(12)]
    me = lax.axis_index("kv")
    my_head = lax.axis_index("head")
    my_y, my_x = me // side, me % side
    reqs, local_len, head_dim = keys.shape
    rows = tokens.shape[1]
    heads = q_gain.shape[0]
    per = reqs // nk
    own = per * drafts
    group = heads * drafts
    scale = 1.0 / math.sqrt(head_dim)
    to_log2 = scale * math.log2(math.e)
    order = [at for batch in batches for at in batch]
    bounds = np.cumsum([0] + [len(batch) for batch in batches]).tolist()

    def ahead(n):
        y, x = order[n]
        return lax.rem(my_y + y, side) * side + lax.rem(my_x + x, side)

    def behind(n):
        y, x = order[n]
        return lax.rem(my_y + side - y, side) * side + lax.rem(my_x + side - x, side)

    def send(src, dst, send_sem, recv_sem, to):
        pltpu.make_async_remote_copy(
            src_ref=src, dst_ref=dst, send_sem=send_sem, recv_sem=recv_sem,
            device_id=to, device_id_type=MESH,
        ).start()

    barrier = pltpu.get_barrier_semaphore()
    for n in range(1, nk):
        pl.semaphore_signal(barrier, inc=1, device_id={"kv": ahead(n)}, device_id_type=MESH)
    for s in range(1, nh):
        pl.semaphore_signal(
            barrier, inc=1, device_id={"head": lax.rem(my_head + s, nh)}, device_id_type=MESH
        )

    loads = [
        pltpu.make_async_copy(src, dst, load_sem.at[n])
        for n, (src, dst) in enumerate(
            [
                (tokens, tok_v), (q_weight, wq_v), (key_matrix, wk_v), (value_matrix, wv_v),
                (q_gain, qg_v), (k_gain, kg_v), (freq, freq_v), (o_weight, wo_v),
                (lengths_in, lengths), (positions_in, positions),
            ]
        )
    ]
    for copy in loads:
        copy.start()
    for b in range(len(batches)):
        for n in range(bounds[b], bounds[b + 1]):
            at = pl.ds(per * behind(n), per)
            slot = pl.ds(per * n, per)
            pltpu.make_async_copy(keys.at[at], keys_v.at[slot], key_sem.at[b]).start()
            pltpu.make_async_copy(values.at[at], values_v.at[slot], value_sem.at[b]).start()

    for copy in loads[:4]:
        copy.wait()
    toks = tok_v[...].T

    def place_part(h, left):
        part[:, h * own : (h + 2) * own, :] = jnp.concatenate(
            [
                left[:, k * head_dim : (k + 1) * head_dim].reshape(nk, own, head_dim)
                for k in range(2)
            ],
            axis=1,
        )

    for h in range(0, heads, 2):
        weight = wq_v[:, h * head_dim : (h + 2) * head_dim]
        place_part(h, jnp.dot(toks, weight, preferred_element_type=jnp.float32))
    weight = jnp.concatenate([wk_v[...], wv_v[...]], axis=1)
    place_part(heads, jnp.dot(toks, weight, preferred_element_type=jnp.float32))

    pl.semaphore_wait(barrier, nk + nh - 2)

    q_rows = pl.ds(0, heads * own)
    kv_rows = pl.ds(heads * own, 2 * own)
    for some, sem in ((q_rows, part_rs), (kv_rows, fresh_rs)):
        for n in range(1, nk):
            send(
                part.at[ahead(n), some], part_in.at[n - 1, some], part_ss, sem,
                {"kv": ahead(n)},
            )

    for copy in loads[4:]:
        copy.wait()
    row_id = lax.broadcasted_iota(jnp.int32, (own, head_dim), 0)
    lane_id = lax.broadcasted_iota(jnp.int32, (own, head_dim), 1)
    place = [[positions[j, per * me + r] for j in range(drafts)] for r in range(per)]
    place_rows = jnp.zeros((own, head_dim), jnp.int32)
    for r in range(per):
        for j in range(drafts):
            place_rows = jnp.where(row_id == r * drafts + j, place[r][j], place_rows)
    angle = place_rows.astype(jnp.float32) * freq_v[...]
    cosine = jnp.cos(angle)
    sine = jnp.sin(angle)
    sine = jnp.where(lane_id < head_dim // 2, -sine, sine)
    fresh_row = lax.broadcasted_iota(jnp.int32, (per * group, 16), 0)
    fresh_col = lax.broadcasted_iota(jnp.int32, (per * group, 16), 1)
    seen = fresh_row < 0
    for r in range(per):
        for j in range(drafts):
            here = (fresh_row // group == r) & (fresh_row % drafts == j)
            for i in range(j + 1):
                hit = here & (fresh_col == r * drafts + i)
                if i < j:
                    hit = hit & (place[r][i] < place[r][j])
                seen = seen | hit

    def norm_rotate(vec, gain):
        vec = vec * lax.rsqrt(jnp.mean(vec * vec, axis=-1, keepdims=True) + EPSILON) * gain
        turned = pltpu.roll(vec.reshape(-1, head_dim), head_dim // 2, 1).reshape(vec.shape)
        return vec * cosine[None] + turned * sine[None]

    def gathered(some):
        raw = part[me, some]
        for n in range(nk - 1):
            raw = raw + part_in[n, some]
        return raw.reshape(-1, own, head_dim)

    drain(part_in.at[:, q_rows], part_rs)
    queries = norm_rotate(gathered(q_rows), qg_v[...][:, None, :])
    queries = jnp.swapaxes(queries.reshape(heads, per, drafts, head_dim), 0, 1)
    queries = queries.reshape(per * group, head_dim).astype(jnp.bfloat16)
    query[0] = queries
    for b in range(len(batches)):
        for n in range(max(bounds[b], 1), bounds[b + 1]):
            send(query.at[0], query.at[n], query_ss, query_rs.at[b], {"kv": ahead(n)})

    drain(part_in.at[:, kv_rows], fresh_rs)
    fresh_kv = gathered(kv_rows)
    fresh_k = norm_rotate(fresh_kv[:1], kg_v[...][:, None, :]).reshape(own, head_dim)
    pad = jnp.zeros((16 - own, head_dim), jnp.float32)
    fresh_k = jnp.concatenate([fresh_k, pad], axis=0).astype(jnp.bfloat16)
    fresh_v = jnp.concatenate([fresh_kv[1], pad], axis=0).astype(jnp.bfloat16)

    def softmax_part(scores, vals):
        top = jnp.max(scores, axis=-1, keepdims=True)
        weights = jnp.exp2((scores - top) * to_log2)
        total = jnp.sum(weights, axis=-1, keepdims=True)
        mixed = jnp.dot(weights.astype(jnp.bfloat16), vals, preferred_element_type=jnp.float32)
        return mixed / total, top * to_log2 + jnp.log2(total)

    def dot_t(left, right):
        return lax.dot_general(
            left, right, (((1,), (1,)), ((), ())), preferred_element_type=jnp.float32
        )

    fresh_out, fresh_lse = softmax_part(
        jnp.where(seen, dot_t(queries, fresh_k), NEG), fresh_v
    )
    fresh_lse = column_to_row(fresh_lse)

    spot = me * local_len + lax.broadcasted_iota(jnp.int32, (1, local_len), 1)
    zero = jnp.zeros((group, head_dim), jnp.bfloat16)

    def rows_of(array, r):
        return array[r * group : (r + 1) * group]

    def attend(n):
        block = query[n]
        wide = jnp.concatenate(
            [
                jnp.concatenate(
                    [rows_of(block, r) if c == r else zero for c in range(per)], axis=1
                )
                for r in range(per)
            ],
            axis=0,
        )
        ks = jnp.concatenate([keys_v[per * n + r] for r in range(per)], axis=1)
        vs = jnp.concatenate([values_v[per * n + r] for r in range(per)], axis=1)
        scores = dot_t(wide, ks)
        scores = jnp.concatenate(
            [
                jnp.where(spot < lengths[per * behind(n) + r], rows_of(scores, r), NEG)
                for r in range(per)
            ],
            axis=0,
        )
        mixed, stat = softmax_part(scores, vs)
        mixed = jnp.concatenate(
            [rows_of(mixed, r)[:, r * head_dim : (r + 1) * head_dim] for r in range(per)], axis=0
        )
        return mixed, stat

    for b in range(len(batches)):
        slots = range(bounds[b], bounds[b + 1])
        away = range(max(bounds[b], 1), bounds[b + 1])
        drain(query.at[pl.ds(away[0], len(away))], query_rs.at[b])
        block = pl.ds(per * slots[0], per * len(slots))
        drain(keys_v.at[block], key_sem.at[b])
        drain(values_v.at[block], value_sem.at[b])
        results = [attend(n) for n in slots]
        for n, (mixed, stat) in zip(slots, results):
            attn[n] = mixed.astype(jnp.bfloat16)
            lse[n] = column_to_row(stat)
        for n in away:
            send(attn.at[n], attn_in.at[n - 1], attn_ss, attn_rs, {"kv": behind(n)})
            send(lse.at[n], lse_in.at[n - 1], lse_ss, lse_rs, {"kv": behind(n)})

    drain(lse_in, lse_rs)
    stats = jnp.concatenate([lse[0], fresh_lse] + [lse_in[n] for n in range(nk - 1)], axis=0)
    ratio = jnp.exp2(stats - jnp.max(stats, axis=0, keepdims=True))
    ratio = ratio / jnp.sum(ratio, axis=0, keepdims=True)
    ratio = jnp.concatenate([ratio, jnp.zeros((128 - nk - 1, 128), jnp.float32)], axis=0).T
    ratio = ratio[: per * group]
    merged = attn[0].astype(jnp.float32) * ratio[:, 0:1] + fresh_out * ratio[:, 1:2]
    drain(attn_in, attn_rs)
    for n in range(nk - 1):
        merged = merged + attn_in[n].astype(jnp.float32) * ratio[:, n + 2 : n + 3]
    merged = jnp.swapaxes(merged.reshape(per, heads, drafts, head_dim), 0, 1)
    attended[me] = merged.reshape(heads * own, head_dim).astype(jnp.bfloat16)
    for n in range(1, nk):
        send(attended.at[me], attended.at[me], att_ss, att_rs, {"kv": ahead(n)})
    drain(attended.at[pl.ds(0, nk - 1)], att_rs)

    total = None
    for h in range(0, heads, 2):
        pair = attended[:, h * own : (h + 2) * own, :].astype(jnp.float32)
        pair = pair.reshape(nk, 2, own, head_dim)
        for k in range(2):
            side_in = pair[:, k].reshape(rows, head_dim).astype(jnp.bfloat16)
            term = dot_t(side_in, wo_v[:, (h + k) * head_dim : (h + k + 1) * head_dim])
            total = term if total is None else total + term
    proj[...] = total.astype(jnp.bfloat16).reshape(proj.shape)
    for s in range(1, nh):
        target = lax.rem(my_head + s, nh)
        send(proj.at[target], proj_in.at[s - 1], proj_ss, proj_rs, {"head": target})
    drain(proj_in, proj_rs)
    result = proj[my_head].astype(jnp.float32)
    for s in range(nh - 1):
        result = result + proj_in[s].astype(jnp.float32)
    out[...] = result.astype(jnp.bfloat16)

    drain(part_in, part_ss)
    drain(attn_in, query_ss)
    drain(attn_in, attn_ss)
    drain(lse_in, lse_ss)
    drain(attn_in, att_ss)
    drain(proj_in, proj_ss)


def on_device(
    nk, nh,
    tokens, q_weight, key_matrix, value_matrix, q_gain, k_gain, keys, values, lengths, positions,
    o_weight,
):
    rows = tokens.shape[0]
    reqs, drafts = positions.shape
    width = o_weight.shape[1]
    tokens, o_weight, positions = tokens.T, o_weight.T, positions.T
    _, local_len, _, head_dim = keys.shape
    keys = keys.reshape(reqs, local_len, head_dim)
    values = values.reshape(reqs, local_len, head_dim)
    heads = q_gain.shape[0]
    side = math.isqrt(nk)
    batches = schedule(side)
    own = rows // nk
    block = rows // nh
    exponent = np.arange(head_dim // 2, dtype=np.float64) * 2.0 / head_dim
    freq = np.tile((ROPE_BASE ** -exponent).astype(np.float32), 2)[None]
    bf16, f32 = jnp.bfloat16, jnp.float32
    dma = pltpu.SemaphoreType.DMA
    hbm = pl.BlockSpec(memory_space=pltpu.HBM)
    return pl.pallas_call(
        functools.partial(kernel, nk, side, nh, drafts, batches),
        out_shape=jax.ShapeDtypeStruct((block, width), bf16),
        in_specs=[hbm] * 12,
        out_specs=pl.BlockSpec(memory_space=pltpu.VMEM),
        scratch_shapes=[
            pltpu.VMEM(tokens.shape, bf16),
            pltpu.VMEM(q_weight.shape, bf16),
            pltpu.VMEM(key_matrix.shape, bf16),
            pltpu.VMEM(value_matrix.shape, bf16),
            pltpu.VMEM(q_gain.shape, f32),
            pltpu.VMEM(k_gain.shape, f32),
            pltpu.VMEM(o_weight.shape, bf16),
            pltpu.VMEM(freq.shape, f32),
            pltpu.VMEM(keys.shape, bf16),
            pltpu.VMEM(values.shape, bf16),
            pltpu.SMEM(lengths.shape, jnp.int32),
            pltpu.SMEM(positions.shape, jnp.int32),
            pltpu.VMEM((nk, (heads + 2) * own, head_dim), f32),
            pltpu.VMEM((nk - 1, (heads + 2) * own, head_dim), f32),
            pltpu.VMEM((nk, heads * own, head_dim), bf16),
            pltpu.VMEM((nk, heads * own, head_dim), bf16),
            pltpu.VMEM((nk - 1, heads * own, head_dim), bf16),
            pltpu.VMEM((nk, 1, 128), f32),
            pltpu.VMEM((nk - 1, 1, 128), f32),
            pltpu.VMEM((nk, heads * own, head_dim), bf16),
            pltpu.VMEM((nh, block, width), bf16),
            pltpu.VMEM((nh - 1, block, width), bf16),
            dma((10,)),
            dma((len(batches),)),
            dma((len(batches),)),
            dma((len(batches),)),
            dma((12,)),
        ],
        compiler_params=pltpu.CompilerParams(
            collective_id=0, has_side_effects=True, vmem_limit_bytes=60 * 1024 * 1024
        ),
    )(
        tokens, q_weight, key_matrix, value_matrix, q_gain, k_gain, keys, values, o_weight,
        jnp.asarray(freq), lengths, positions,
    )


def solution(mesh):
    placed = (
        P(None, "kv"),
        P("kv", "head"),
        P("kv", "head"),
        P("kv", "head"),
        P("head", None),
        P("head", None),
        P(None, "kv", "head", None),
        P(None, "kv", "head", None),
        P(),
        P(),
        P("head", "kv"),
    )
    return jax.shard_map(
        functools.partial(on_device, mesh.shape["kv"], mesh.shape["head"]),
        mesh=mesh,
        in_specs=placed,
        out_specs=P("head", "kv"),
        check_vma=False,
    )
```

time: 53.2 us -> 47.3 us (0.89)
  Pallas kernels: 51.7 us -> 45.9 us
    pallas_call x1, Pallas kernels: 51.7 us -> 45.9 us  [on_device(): pl.pallas_call(functools.partial(kernel, nk, side, nh, drafts, batches),...]
where the time goes in v2:
time: 47.3 us; the launch traced here: 47.2 us
  Pallas kernels  45.9 us (97%)
  local copies, waits for them, and re-layouts  1.31 us (3%)
    pallas_call x1, Pallas kernels, on_device(): pl.pallas_call(functools.partial(kernel, nk, side, nh, drafts, batches),...  45.9 us
    unnamed x1, local copies, waits for them, and re-layouts  1.31 us

profile of v2, /device:TPU:1, one launch (start us, length us, event | category | flops | bytes accessed | tf_op | source)
XLA Modules:
  0.0 47.2 jit_solution(12480665850091529496)
XLA Ops:
  0.0 45.9 %shard_map.118 = bf16[16,320]{1,0:T(8,128)(2,1)} custom-call(bf16[320,128]{1,0:T(8,128)(2,1)} %bitcast.8, bf16[320,1024]{1,0:T(8,128)(2,1)} %q_weight.1, bf16[320,128]{1,0:T(8,128)(2,1)} %key_matrix.1, bf16[320,128]{1,0:T(8,128)(2,1)} %value_matrix.1, f32[8,128]{1,0:T(8,128)} %q_gain.1, f32[1,128]{1,0:T(1,128)} %k_gain.1, bf16[32,1024,128]{2,1,0:T(8,128)(2,1)} %bitcast.5, ...), custom_call_target="tpu_custom_call" | custom-call | tf_op jit(solution)/shard_map/pallas_call | solution.py:320
  45.9 1.3 %copy.14 = bf16[16,320]{1,0:T(8,128)(2,1)} copy(bf16[16,320]{1,0:T(8,128)(2,1)} %shard_map.118) | data formatting | bytes 20480

commit v3 on v2

v3 whole, which is shorter than its diff:
```python
import functools
import math

import jax
import jax.numpy as jnp
import numpy as np
from jax import lax
from jax.experimental import pallas as pl
from jax.experimental.pallas import tpu as pltpu
from jax.sharding import PartitionSpec as P

EPSILON = 1e-06
ROPE_BASE = 1000000.0
NEG = -1e30
MESH = pl.DeviceIdType.MESH


def column_to_row(col, first):
    rows = col.shape[0]
    wide = jnp.broadcast_to(col, (rows, 128))
    row_id = lax.broadcasted_iota(jnp.int32, (rows, 128), 0)
    lane_id = lax.broadcasted_iota(jnp.int32, (rows, 128), 1)
    return jnp.sum(jnp.where(row_id + first == lane_id, wide, 0.0), axis=0, keepdims=True)


def by_distance(side):
    spots = [(y, x) for y in range(side) for x in range(side)]
    return sorted(spots, key=lambda at: sum(min(d, side - d) for d in at))


def drain(ref, sem):
    pltpu.make_async_copy(ref, ref, sem).wait()


def kernel(
    nk, side, nh, drafts,
    tokens, q_weight, key_matrix, value_matrix, q_gain, k_gain, keys, values, o_weight, freq,
    lengths_in, positions_in,
    out,
    tok_v, wq_v, wk_v, wv_v, qg_v, kg_v, wo_v, freq_v, keys_v, values_v, lengths, positions,
    part, part_in, fresh, fresh_in, query, attn, attn_in, lse, lse_in, attended, proj, proj_in,
    load_sem, key_sem, value_sem, part_rs, query_rs, sems,
):
    (part_ss, fresh_ss, fresh_rs, query_ss, attn_ss, attn_rs, lse_ss, lse_rs, att_ss, att_rs,
     proj_ss, proj_rs) = [sems.at[n] for n in range(12)]
    me = lax.axis_index("kv")
    my_head = lax.axis_index("head")
    my_y, my_x = me // side, me % side
    reqs, local_len, head_dim = keys.shape
    rows = tokens.shape[1]
    heads = q_gain.shape[0]
    per = reqs // nk
    own = per * drafts
    group = heads * drafts
    scale = 1.0 / math.sqrt(head_dim)
    to_log2 = scale * math.log2(math.e)
    order = by_distance(side)
    half = nk // 2

    def ahead(n):
        y, x = order[n]
        return lax.rem(my_y + y, side) * side + lax.rem(my_x + x, side)

    def behind(n):
        y, x = order[n]
        return lax.rem(my_y + side - y, side) * side + lax.rem(my_x + side - x, side)

    def send(src, dst, send_sem, recv_sem, to):
        pltpu.make_async_remote_copy(
            src_ref=src, dst_ref=dst, send_sem=send_sem, recv_sem=recv_sem,
            device_id=to, device_id_type=MESH,
        ).start()

    barrier = pltpu.get_barrier_semaphore()
    for n in reversed(range(1, nk)):
        pl.semaphore_signal(barrier, inc=1, device_id={"kv": ahead(n)}, device_id_type=MESH)
    for s in range(1, nh):
        pl.semaphore_signal(
            barrier, inc=1, device_id={"head": lax.rem(my_head + s, nh)}, device_id_type=MESH
        )

    loads = [
        pltpu.make_async_copy(src, dst, load_sem.at[n])
        for n, (src, dst) in enumerate(
            [
                (tokens, tok_v), (q_weight, wq_v), (key_matrix, wk_v), (value_matrix, wv_v),
                (q_gain, qg_v), (k_gain, kg_v), (freq, freq_v), (o_weight, wo_v),
                (lengths_in, lengths), (positions_in, positions),
            ]
        )
    ]
    for copy in loads[:4]:
        copy.start()
    for copy in loads[:4]:
        copy.wait()
    toks = tok_v[...].T

    upper = lax.broadcasted_iota(jnp.int32, (rows, head_dim), 0) % own < drafts

    def split(first, second):
        low = jnp.where(upper, first, pltpu.roll(second, drafts, 0))
        high = jnp.where(upper, pltpu.roll(first, rows - drafts, 0), second)
        return [low.reshape(nk, own, head_dim), high.reshape(nk, own, head_dim)]

    for h in range(0, heads, 2):
        weight = wq_v[:, h * head_dim : (h + 2) * head_dim]
        both = jnp.dot(toks, weight, preferred_element_type=jnp.float32)
        for r, piece in enumerate(split(both[:, :head_dim], both[:, head_dim:])):
            part[r, :, h * drafts : (h + 2) * drafts, :] = piece
    weight = jnp.concatenate([wk_v[...], wv_v[...]], axis=1)
    both = jnp.dot(toks, weight, preferred_element_type=jnp.float32)
    fresh[...] = jnp.concatenate(
        [both[:, k * head_dim : (k + 1) * head_dim].reshape(nk, own, head_dim) for k in range(2)],
        axis=1,
    )

    pl.semaphore_wait(barrier, nk + nh - 2)

    for r in range(per):
        for n in range(1, nk):
            send(
                part.at[r, ahead(n)], part_in.at[r, n - 1], part_ss, part_rs.at[r],
                {"kv": ahead(n)},
            )
    for n in range(1, nk):
        send(fresh.at[ahead(n)], fresh_in.at[n - 1], fresh_ss, fresh_rs, {"kv": ahead(n)})

    for copy in loads[4:]:
        copy.start()
    for r in range(per):
        for b in ((0, 1), (1, 0))[r]:
            for n in range(b * half, (b + 1) * half):
                at = per * behind(n) + r
                pltpu.make_async_copy(
                    keys.at[at], keys_v.at[r * nk + n], key_sem.at[2 * r + b]
                ).start()
                pltpu.make_async_copy(
                    values.at[at], values_v.at[r * nk + n], value_sem.at[2 * r + b]
                ).start()
    for copy in loads[4:]:
        copy.wait()
    row_id = lax.broadcasted_iota(jnp.int32, (own, head_dim), 0)
    lane_id = lax.broadcasted_iota(jnp.int32, (own, head_dim), 1)
    place = [[positions[j, per * me + r] for j in range(drafts)] for r in range(per)]
    place_rows = jnp.zeros((own, head_dim), jnp.int32)
    for r in range(per):
        for j in range(drafts):
            place_rows = jnp.where(row_id == r * drafts + j, place[r][j], place_rows)
    angle = place_rows.astype(jnp.float32) * freq_v[...]
    cosine = jnp.cos(angle)
    sine = jnp.sin(angle)
    sine = jnp.where(lane_id < head_dim // 2, -sine, sine)
    fresh_row = lax.broadcasted_iota(jnp.int32, (per * group, 16), 0)
    fresh_col = lax.broadcasted_iota(jnp.int32, (per * group, 16), 1)
    seen = fresh_row < 0
    for r in range(per):
        for j in range(drafts):
            here = (fresh_row // group == r) & (fresh_row % drafts == j)
            for i in range(j + 1):
                hit = here & (fresh_col == r * drafts + i)
                if i < j:
                    hit = hit & (place[r][i] < place[r][j])
                seen = seen | hit

    top_half = row_id < drafts

    def spread(array, r):
        turned = pltpu.roll(array, drafts, 0)
        return jnp.where(top_half, array, turned) if r == 0 else jnp.where(top_half, turned, array)

    turns = [(spread(cosine, r)[None], spread(sine, r)[None]) for r in range(per)]
    gains = qg_v[...]
    gains = jnp.concatenate(
        [
            jnp.where(top_half, gains[h : h + 1], gains[h + 1 : h + 2])[None]
            for h in range(0, heads, 2)
        ],
        axis=0,
    )

    def norm_rotate(vec, gain, turn):
        vec = vec * lax.rsqrt(jnp.mean(vec * vec, axis=-1, keepdims=True) + EPSILON) * gain
        turned = pltpu.roll(vec.reshape(-1, head_dim), head_dim // 2, 1).reshape(vec.shape)
        return vec * turn[0] + turned * turn[1]

    queries = []
    for r in range(per):
        drain(part_in.at[r], part_rs.at[r])
        raw = part[r, me]
        for n in range(nk - 1):
            raw = raw + part_in[r, n]
        mine = norm_rotate(raw.reshape(heads // 2, own, head_dim), gains, turns[r])
        mine = mine.reshape(group, head_dim).astype(jnp.bfloat16)
        queries.append(mine)
        query[r, 0] = mine
        for b in ((0, 1), (1, 0))[r]:
            for n in range(max(b * half, 1), (b + 1) * half):
                send(
                    query.at[r, 0], query.at[r, n], query_ss, query_rs.at[2 * r + b],
                    {"kv": ahead(n)},
                )
    queries = jnp.concatenate(queries, axis=0)

    drain(fresh_in, fresh_rs)
    fresh_kv = fresh[me]
    for n in range(nk - 1):
        fresh_kv = fresh_kv + fresh_in[n]
    fresh_k = norm_rotate(fresh_kv[:own][None], kg_v[...], (cosine[None], sine[None]))
    pad = jnp.zeros((16 - own, head_dim), jnp.float32)
    fresh_k = jnp.concatenate([fresh_k.reshape(own, head_dim), pad], axis=0).astype(jnp.bfloat16)
    fresh_v = jnp.concatenate([fresh_kv[own:], pad], axis=0).astype(jnp.bfloat16)

    def softmax_part(scores, vals):
        top = jnp.max(scores, axis=-1, keepdims=True)
        weights = jnp.exp2((scores - top) * to_log2)
        total = jnp.sum(weights, axis=-1, keepdims=True)
        mixed = jnp.dot(weights.astype(jnp.bfloat16), vals, preferred_element_type=jnp.float32)
        return mixed / total, top * to_log2 + jnp.log2(total)

    def dot_t(left, right):
        return lax.dot_general(
            left, right, (((1,), (1,)), ((), ())), preferred_element_type=jnp.float32
        )

    fresh_out, fresh_lse = softmax_part(
        jnp.where(seen, dot_t(queries, fresh_k), NEG), fresh_v
    )
    fresh_lse = column_to_row(fresh_lse, 0)

    spot = me * local_len + lax.broadcasted_iota(jnp.int32, (1, local_len), 1)
    zero = jnp.zeros((group, head_dim), jnp.bfloat16)

    def rows_of(array, r):
        return array[r * group : (r + 1) * group]

    def attend(r, n):
        wide = jnp.concatenate(
            [
                jnp.concatenate([query[r, n], zero], axis=1),
                jnp.concatenate([zero, query[r, n + 1]], axis=1),
            ],
            axis=0,
        )
        at = r * nk + n
        scores = dot_t(wide, jnp.concatenate([keys_v[at], keys_v[at + 1]], axis=1))
        scores = jnp.concatenate(
            [
                jnp.where(spot < lengths[per * behind(n + k) + r], rows_of(scores, k), NEG)
                for k in range(2)
            ],
            axis=0,
        )
        mixed, stat = softmax_part(
            scores, jnp.concatenate([values_v[at], values_v[at + 1]], axis=1)
        )
        return [
            (rows_of(mixed, k)[:, k * head_dim : (k + 1) * head_dim], rows_of(stat, k))
            for k in range(2)
        ]

    for r in range(per):
        for b in ((0, 1), (1, 0))[r]:
            slots = range(b * half, (b + 1) * half)
            away = slots[1:] if b == 0 else slots
            drain(query.at[r, pl.ds(away[0], len(away))], query_rs.at[2 * r + b])
            block = pl.ds(r * nk + b * half, half)
            drain(keys_v.at[block], key_sem.at[2 * r + b])
            drain(values_v.at[block], value_sem.at[2 * r + b])
            results = [part_of for n in slots[::2] for part_of in attend(r, n)]
            for n, (mixed, stat) in zip(slots, results):
                attn[r, n] = mixed.astype(jnp.bfloat16)
                if r == 0:
                    lse[n] = column_to_row(stat, 0)
                else:
                    lse[n] = lse[n] + column_to_row(stat, group)
            for n in away:
                send(attn.at[r, n], attn_in.at[r, n - 1], attn_ss, attn_rs, {"kv": behind(n)})
                if r == per - 1:
                    send(lse.at[n], lse_in.at[n - 1], lse_ss, lse_rs, {"kv": behind(n)})

    drain(lse_in, lse_rs)
    stats = jnp.concatenate([lse[0], fresh_lse] + [lse_in[n] for n in range(nk - 1)], axis=0)
    ratio = jnp.exp2(stats - jnp.max(stats, axis=0, keepdims=True))
    ratio = ratio / jnp.sum(ratio, axis=0, keepdims=True)
    ratio = jnp.concatenate([ratio, jnp.zeros((128 - nk - 1, 128), jnp.float32)], axis=0).T
    ratio = ratio[: per * group]
    merged = attn[:, 0].astype(jnp.float32).reshape(per * group, head_dim) * ratio[:, 0:1] + fresh_out * ratio[:, 1:2]
    drain(attn_in, attn_rs)
    for n in range(nk - 1):
        piece = attn_in[:, n].astype(jnp.float32).reshape(per * group, head_dim)
        merged = merged + piece * ratio[:, n + 2 : n + 3]
    merged = jnp.swapaxes(merged.reshape(per, heads, drafts, head_dim), 0, 1)
    merged = merged.reshape(heads, own, head_dim)
    attended[me] = jnp.concatenate(
        [
            jnp.concatenate([merged[h + k * heads // 2] for h in range(heads // 2)], axis=1)
            for k in range(2)
        ],
        axis=0,
    ).astype(jnp.bfloat16)
    for n in range(1, nk):
        send(attended.at[me], attended.at[me], att_ss, att_rs, {"kv": ahead(n)})
    drain(attended.at[pl.ds(0, nk - 1)], att_rs)

    everyone = attended[...].reshape(nk * 2 * own, heads * head_dim // 2)
    total = None
    for k in range(2):
        half = pl.ds(k * heads * head_dim // 2, heads * head_dim // 2)
        term = dot_t(everyone, wo_v[:, half]).reshape(nk, 2, own, -1)[:, k]
        total = term if total is None else total + term
    width = out.shape[1]
    spare = jnp.zeros((rows, proj.shape[2] - width), jnp.float32)
    total = jnp.concatenate([total.reshape(rows, width), spare], axis=1)
    proj[...] = total.astype(jnp.bfloat16).reshape(proj.shape)
    for s in range(1, nh):
        target = lax.rem(my_head + s, nh)
        send(proj.at[target], proj_in.at[s - 1], proj_ss, proj_rs, {"head": target})
    drain(proj_in, proj_rs)
    result = proj[my_head].astype(jnp.float32)
    for s in range(nh - 1):
        result = result + proj_in[s].astype(jnp.float32)
    out[...] = result[:, :width].astype(jnp.bfloat16)

    drain(part_in, part_ss)
    drain(fresh_in, fresh_ss)
    drain(attn_in, query_ss)
    drain(attn_in, attn_ss)
    drain(lse_in, lse_ss)
    drain(attended.at[pl.ds(0, nk - 1)], att_ss)
    drain(proj_in, proj_ss)


def on_device(
    nk, nh,
    tokens, q_weight, key_matrix, value_matrix, q_gain, k_gain, keys, values, lengths, positions,
    o_weight,
):
    rows = tokens.shape[0]
    reqs, drafts = positions.shape
    width = o_weight.shape[1]
    tokens, o_weight, positions = tokens.T, o_weight.T, positions.T
    _, local_len, _, head_dim = keys.shape
    keys = keys.reshape(reqs, local_len, head_dim)
    values = values.reshape(reqs, local_len, head_dim)
    heads = q_gain.shape[0]
    side = math.isqrt(nk)
    own = rows // nk
    per = reqs // nk
    group = heads * drafts
    block = rows // nh
    padded = -(-width // 128) * 128
    exponent = np.arange(head_dim // 2, dtype=np.float64) * 2.0 / head_dim
    freq = np.tile((ROPE_BASE ** -exponent).astype(np.float32), 2)[None]
    bf16, f32 = jnp.bfloat16, jnp.float32
    dma = pltpu.SemaphoreType.DMA
    hbm = pl.BlockSpec(memory_space=pltpu.HBM)
    return pl.pallas_call(
        functools.partial(kernel, nk, side, nh, drafts),
        out_shape=jax.ShapeDtypeStruct((block, width), bf16),
        in_specs=[hbm] * 12,
        out_specs=pl.BlockSpec(memory_space=pltpu.VMEM),
        scratch_shapes=[
            pltpu.VMEM(tokens.shape, bf16),
            pltpu.VMEM(q_weight.shape, bf16),
            pltpu.VMEM(key_matrix.shape, bf16),
            pltpu.VMEM(value_matrix.shape, bf16),
            pltpu.VMEM(q_gain.shape, f32),
            pltpu.VMEM(k_gain.shape, f32),
            pltpu.VMEM(o_weight.shape, bf16),
            pltpu.VMEM(freq.shape, f32),
            pltpu.VMEM(keys.shape, bf16),
            pltpu.VMEM(values.shape, bf16),
            pltpu.SMEM(lengths.shape, jnp.int32),
            pltpu.SMEM(positions.shape, jnp.int32),
            pltpu.VMEM((per, nk, group, head_dim), f32),
            pltpu.VMEM((per, nk - 1, group, head_dim), f32),
            pltpu.VMEM((nk, 2 * own, head_dim), f32),
            pltpu.VMEM((nk - 1, 2 * own, head_dim), f32),
            pltpu.VMEM((per, nk, group, head_dim), bf16),
            pltpu.VMEM((per, nk, group, head_dim), bf16),
            pltpu.VMEM((per, nk - 1, group, head_dim), bf16),
            pltpu.VMEM((nk, 1, 128), f32),
            pltpu.VMEM((nk - 1, 1, 128), f32),
            pltpu.VMEM((nk, 2 * own, heads * head_dim // 2), bf16),
            pltpu.VMEM((nh, block, padded), bf16),
            pltpu.VMEM((nh - 1, block, padded), bf16),
            dma((10,)),
            dma((2 * per,)),
            dma((2 * per,)),
            dma((per,)),
            dma((2 * per,)),
            dma((12,)),
        ],
        compiler_params=pltpu.CompilerParams(
            collective_id=0, has_side_effects=True, vmem_limit_bytes=60 * 1024 * 1024
        ),
    )(
        tokens, q_weight, key_matrix, value_matrix, q_gain, k_gain, keys, values, o_weight,
        jnp.asarray(freq), lengths, positions,
    )


def solution(mesh):
    placed = (
        P(None, "kv"),
        P("kv", "head"),
        P("kv", "head"),
        P("kv", "head"),
        P("head", None),
        P("head", None),
        P(None, "kv", "head", None),
        P(None, "kv", "head", None),
        P(),
        P(),
        P("head", "kv"),
    )
    return jax.shard_map(
        functools.partial(on_device, mesh.shape["kv"], mesh.shape["head"]),
        mesh=mesh,
        in_specs=placed,
        out_specs=P("head", "kv"),
        check_vma=False,
    )
```

time: 47.3 us -> 45.3 us (0.958)
  Pallas kernels: 45.9 us -> 43.8 us
    pallas_call x1, Pallas kernels: 45.9 us -> 43.8 us  [on_device(): pl.pallas_call(functools.partial(kernel, nk, side, nh, drafts), out_shape...]
where the time goes in v3:
time: 45.3 us; the launch traced here: 45.1 us
  Pallas kernels  43.8 us (97%)
  local copies, waits for them, and re-layouts  1.31 us (3%)
    pallas_call x1, Pallas kernels, on_device(): pl.pallas_call(functools.partial(kernel, nk, side, nh, drafts), out_shape...  43.8 us
    unnamed x1, local copies, waits for them, and re-layouts  1.31 us

profile of v3, /device:TPU:1, one launch (start us, length us, event | category | flops | bytes accessed | tf_op | source)
XLA Modules:
  0.0 45.1 jit_solution(17862769459792188417)
XLA Ops:
  0.0 43.8 %shard_map.118 = bf16[16,320]{1,0:T(8,128)(2,1)} custom-call(bf16[320,128]{1,0:T(8,128)(2,1)} %bitcast.8, bf16[320,1024]{1,0:T(8,128)(2,1)} %q_weight.1, bf16[320,128]{1,0:T(8,128)(2,1)} %key_matrix.1, bf16[320,128]{1,0:T(8,128)(2,1)} %value_matrix.1, f32[8,128]{1,0:T(8,128)} %q_gain.1, f32[1,128]{1,0:T(1,128)} %k_gain.1, bf16[32,1024,128]{2,1,0:T(8,128)(2,1)} %bitcast.5, ...), custom_call_target="tpu_custom_call" | custom-call | tf_op jit(solution)/shard_map/pallas_call | solution.py:357
  43.8 1.3 %copy.14 = bf16[16,320]{1,0:T(8,128)(2,1)} copy(bf16[16,320]{1,0:T(8,128)(2,1)} %shard_map.118) | data formatting | bytes 20480

commit v4 on v3

--- a/solution.py
+++ b/solution.py
@@ -55,7 +55,11 @@
     scale = 1.0 / math.sqrt(head_dim)
     to_log2 = scale * math.log2(math.e)
     order = by_distance(side)
-    half = nk // 2
+    quarter = max(nk // 4, 2)
+    spans = [(0, quarter), (quarter, 2 * quarter), (2 * quarter, nk)]
+    spans = [span for span in spans if span[0] < span[1]]
+    stages = [spans, spans[::-1]]
+    steps = len(stages[0])
 
     def ahead(n):
         y, x = order[n]
@@ -128,14 +132,14 @@
     for copy in loads[4:]:
         copy.start()
     for r in range(per):
-        for b in ((0, 1), (1, 0))[r]:
-            for n in range(b * half, (b + 1) * half):
+        for b, (low, high) in enumerate(stages[r]):
+            for n in range(low, high):
                 at = per * behind(n) + r
                 pltpu.make_async_copy(
-                    keys.at[at], keys_v.at[r * nk + n], key_sem.at[2 * r + b]
+                    keys.at[at], keys_v.at[r * nk + n], key_sem.at[steps * r + b]
                 ).start()
                 pltpu.make_async_copy(
-                    values.at[at], values_v.at[r * nk + n], value_sem.at[2 * r + b]
+                    values.at[at], values_v.at[r * nk + n], value_sem.at[steps * r + b]
                 ).start()
     for copy in loads[4:]:
         copy.wait()
@@ -193,10 +197,10 @@
         mine = mine.reshape(group, head_dim).astype(jnp.bfloat16)
         queries.append(mine)
         query[r, 0] = mine
-        for b in ((0, 1), (1, 0))[r]:
-            for n in range(max(b * half, 1), (b + 1) * half):
+        for b, (low, high) in enumerate(stages[r]):
+            for n in range(max(low, 1), high):
                 send(
-                    query.at[r, 0], query.at[r, n], query_ss, query_rs.at[2 * r + b],
+                    query.at[r, 0], query.at[r, n], query_ss, query_rs.at[steps * r + b],
                     {"kv": ahead(n)},
                 )
     queries = jnp.concatenate(queries, axis=0)
@@ -259,13 +263,13 @@
         ]
 
     for r in range(per):
-        for b in ((0, 1), (1, 0))[r]:
-            slots = range(b * half, (b + 1) * half)
-            away = slots[1:] if b == 0 else slots
-            drain(query.at[r, pl.ds(away[0], len(away))], query_rs.at[2 * r + b])
-            block = pl.ds(r * nk + b * half, half)
-            drain(keys_v.at[block], key_sem.at[2 * r + b])
-            drain(values_v.at[block], value_sem.at[2 * r + b])
+        for b, (low, high) in enumerate(stages[r]):
+            slots = range(low, high)
+            away = slots[1:] if low == 0 else slots
+            drain(query.at[r, pl.ds(away[0], len(away))], query_rs.at[steps * r + b])
+            block = pl.ds(r * nk + low, high - low)
+            drain(keys_v.at[block], key_sem.at[steps * r + b])
+            drain(values_v.at[block], value_sem.at[steps * r + b])
             results = [part_of for n in slots[::2] for part_of in attend(r, n)]
             for n, (mixed, stat) in zip(slots, results):
                 attn[r, n] = mixed.astype(jnp.bfloat16)
@@ -273,7 +277,7 @@
                     lse[n] = column_to_row(stat, 0)
                 else:
                     lse[n] = lse[n] + column_to_row(stat, group)
-            for n in away:
+            for n in reversed(away):
                 send(attn.at[r, n], attn_in.at[r, n - 1], attn_ss, attn_rs, {"kv": behind(n)})
                 if r == per - 1:
                     send(lse.at[n], lse_in.at[n - 1], lse_ss, lse_rs, {"kv": behind(n)})
@@ -298,7 +302,7 @@
         ],
         axis=0,
     ).astype(jnp.bfloat16)
-    for n in range(1, nk):
+    for n in reversed(range(1, nk)):
         send(attended.at[me], attended.at[me], att_ss, att_rs, {"kv": ahead(n)})
     drain(attended.at[pl.ds(0, nk - 1)], att_rs)
 
@@ -385,10 +389,10 @@
             pltpu.VMEM((nh, block, padded), bf16),
             pltpu.VMEM((nh - 1, block, padded), bf16),
             dma((10,)),
-            dma((2 * per,)),
-            dma((2 * per,)),
+            dma((3 * per,)),
+            dma((3 * per,)),
             dma((per,)),
-            dma((2 * per,)),
+            dma((3 * per,)),
             dma((12,)),
         ],
         compiler_params=pltpu.CompilerParams(

time: 45.3 us -> 43.9 us (0.969)
  Pallas kernels: 43.8 us -> 42.4 us
    pallas_call x1, Pallas kernels: 43.8 us -> 42.4 us  [on_device(): pl.pallas_call(functools.partial(kernel, nk, side, nh, drafts), out_shape...]
where the time goes in v4:
time: 43.9 us; the launch traced here: 43.7 us
  Pallas kernels  42.4 us (97%)
  local copies, waits for them, and re-layouts  1.31 us (3%)
    pallas_call x1, Pallas kernels, on_device(): pl.pallas_call(functools.partial(kernel, nk, side, nh, drafts), out_shape...  42.4 us
    unnamed x1, local copies, waits for them, and re-layouts  1.31 us

profile of v4, /device:TPU:1, one launch (start us, length us, event | category | flops | bytes accessed | tf_op | source)
XLA Modules:
  0.0 43.7 jit_solution(8853008740471871403)
XLA Ops:
  0.0 42.4 %shard_map.118 = bf16[16,320]{1,0:T(8,128)(2,1)} custom-call(bf16[320,128]{1,0:T(8,128)(2,1)} %bitcast.8, bf16[320,1024]{1,0:T(8,128)(2,1)} %q_weight.1, bf16[320,128]{1,0:T(8,128)(2,1)} %key_matrix.1, bf16[320,128]{1,0:T(8,128)(2,1)} %value_matrix.1, f32[8,128]{1,0:T(8,128)} %q_gain.1, f32[1,128]{1,0:T(1,128)} %k_gain.1, bf16[32,1024,128]{2,1,0:T(8,128)(2,1)} %bitcast.5, ...), custom_call_target="tpu_custom_call" | custom-call | tf_op jit(solution)/shard_map/pallas_call | solution.py:361
  42.4 1.3 %copy.14 = bf16[16,320]{1,0:T(8,128)(2,1)} copy(bf16[16,320]{1,0:T(8,128)(2,1)} %shard_map.118) | data formatting | bytes 20480

commit v5 on v4

--- a/solution.py
+++ b/solution.py
@@ -203,6 +203,18 @@
                     query.at[r, 0], query.at[r, n], query_ss, query_rs.at[steps * r + b],
                     {"kv": ahead(n)},
                 )
+    def softmax_part(scores, vals):
+        top = jnp.max(scores, axis=-1, keepdims=True)
+        weights = jnp.exp2((scores - top) * to_log2)
+        total = jnp.sum(weights, axis=-1, keepdims=True)
+        mixed = jnp.dot(weights.astype(jnp.bfloat16), vals, preferred_element_type=jnp.float32)
+        return mixed / total, top * to_log2 + jnp.log2(total)
+
+    def dot_t(left, right):
+        return lax.dot_general(
+            left, right, (((1,), (1,)), ((), ())), preferred_element_type=jnp.float32
+        )
+
     queries = jnp.concatenate(queries, axis=0)
 
     drain(fresh_in, fresh_rs)
@@ -213,18 +225,6 @@
     pad = jnp.zeros((16 - own, head_dim), jnp.float32)
     fresh_k = jnp.concatenate([fresh_k.reshape(own, head_dim), pad], axis=0).astype(jnp.bfloat16)
     fresh_v = jnp.concatenate([fresh_kv[own:], pad], axis=0).astype(jnp.bfloat16)
-
-    def softmax_part(scores, vals):
-        top = jnp.max(scores, axis=-1, keepdims=True)
-        weights = jnp.exp2((scores - top) * to_log2)
-        total = jnp.sum(weights, axis=-1, keepdims=True)
-        mixed = jnp.dot(weights.astype(jnp.bfloat16), vals, preferred_element_type=jnp.float32)
-        return mixed / total, top * to_log2 + jnp.log2(total)
-
-    def dot_t(left, right):
-        return lax.dot_general(
-            left, right, (((1,), (1,)), ((), ())), preferred_element_type=jnp.float32
-        )
 
     fresh_out, fresh_lse = softmax_part(
         jnp.where(seen, dot_t(queries, fresh_k), NEG), fresh_v
@@ -277,10 +277,10 @@
                     lse[n] = column_to_row(stat, 0)
                 else:
                     lse[n] = lse[n] + column_to_row(stat, group)
+            for n in reversed(away) if r == per - 1 else ():
+                send(lse.at[n], lse_in.at[n - 1], lse_ss, lse_rs, {"kv": behind(n)})
             for n in reversed(away):
                 send(attn.at[r, n], attn_in.at[r, n - 1], attn_ss, attn_rs, {"kv": behind(n)})
-                if r == per - 1:
-                    send(lse.at[n], lse_in.at[n - 1], lse_ss, lse_rs, {"kv": behind(n)})
 
     drain(lse_in, lse_rs)
     stats = jnp.concatenate([lse[0], fresh_lse] + [lse_in[n] for n in range(nk - 1)], axis=0)
@@ -316,7 +316,7 @@
     spare = jnp.zeros((rows, proj.shape[2] - width), jnp.float32)
     total = jnp.concatenate([total.reshape(rows, width), spare], axis=1)
     proj[...] = total.astype(jnp.bfloat16).reshape(proj.shape)
-    for s in range(1, nh):
+    for s in sorted(range(1, nh), key=lambda s: abs(s - nh // 2)):
         target = lax.rem(my_head + s, nh)
         send(proj.at[target], proj_in.at[s - 1], proj_ss, proj_rs, {"head": target})
     drain(proj_in, proj_rs)

time: 43.9 us -> 43.6 us (level)
  no operation moved by 1% of the time
where the time goes in v5:
time: 43.6 us; the launch traced here: 43.4 us
  Pallas kernels  42.1 us (97%)
  local copies, waits for them, and re-layouts  1.31 us (3%)
    pallas_call x1, Pallas kernels, on_device(): pl.pallas_call(functools.partial(kernel, nk, side, nh, drafts), out_shape...  42.1 us
    unnamed x1, local copies, waits for them, and re-layouts  1.31 us

profile of v5, /device:TPU:1, one launch (start us, length us, event | category | flops | bytes accessed | tf_op | source)
XLA Modules:
  0.0 43.4 jit_solution(369000437010985276)
XLA Ops:
  0.0 42.1 %shard_map.118 = bf16[16,320]{1,0:T(8,128)(2,1)} custom-call(bf16[320,128]{1,0:T(8,128)(2,1)} %bitcast.8, bf16[320,1024]{1,0:T(8,128)(2,1)} %q_weight.1, bf16[320,128]{1,0:T(8,128)(2,1)} %key_matrix.1, bf16[320,128]{1,0:T(8,128)(2,1)} %value_matrix.1, f32[8,128]{1,0:T(8,128)} %q_gain.1, f32[1,128]{1,0:T(1,128)} %k_gain.1, bf16[32,1024,128]{2,1,0:T(8,128)(2,1)} %bitcast.5, ...), custom_call_target="tpu_custom_call" | custom-call | tf_op jit(solution)/shard_map/pallas_call | solution.py:361
  42.1 1.3 %copy.14 = bf16[16,320]{1,0:T(8,128)(2,1)} copy(bf16[16,320]{1,0:T(8,128)(2,1)} %shard_map.118) | data formatting | bytes 20480
